TPU v7x, 32 devices: a whole 2x2x4 slice. The times are simulated.
32 devices in a mesh: grp: 1, ffn: 8 (over z, core), tok: 4 (over y, x).
Axes of the slice: x: 2, y: 2, z: 4, core: 2. Of those that a mesh axis runs over, the one named last changes fastest.
Arguments:
- tokens: bfloat16 [1024, 16384], P(('grp', 'tok'), 'ffn'), may hold values from -6 to 6
- gate_blocks: bfloat16 [1024, 53248], P(('grp', 'tok'), 'ffn'), may hold values from -0.1875 to 0.1875
- up_blocks: bfloat16 [1024, 53248], P(('grp', 'tok'), 'ffn'), may hold values from -0.1875 to 0.1875
- block_rows: int32 [416, 8], P(('grp', 'ffn')), may hold values from 0 to 127, all different within a row
- slab_offset: int32 [1], P('grp'), may hold values from 0 to 49152, as said below
Outputs:
- hessian_slab: float32 [4096, 53248], P(('grp', 'tok'), 'ffn')
Inputs may be any that keep to these rules, and one draw needn't show every extreme that they name: `block_rows`: each row holds 8 different row-block numbers, and every row-block number appears somewhere. `slab_offset`: a multiple of 128.
All inputs are finite; a program needn't handle non-finite values.
Results may differ from a plain program's by a relative error of at most 0.004.
Values may be sent and summed in bfloat16 or wider, within the bound.
A program may use at most 192 MiB of HBM per device.

v0:
```python
import jax
import jax.numpy as jnp
from jax import lax
from jax.sharding import PartitionSpec as P

BLOCK = 128
SLAB = 4096


def shards(tokens, gate_blocks, up_blocks, block_rows, slab_offset):
    rows_here = tokens.shape[0]
    column_count = block_rows.shape[0]
    whole = lax.all_gather(tokens, "ffn", axis=1, tiled=True)
    feature_tiles = whole.reshape(rows_here, -1, BLOCK)
    chosen_entries = jnp.take(feature_tiles, block_rows, axis=1)
    pieces = (
        lax.all_gather(gate_blocks, "tok", axis=0, tiled=True),
        lax.all_gather(up_blocks, "tok", axis=0, tiled=True),
    )
    block_count = pieces[0].shape[0] // BLOCK
    gate_segment = pieces[0].reshape(block_count, BLOCK, column_count, BLOCK)
    up_segment = pieces[1].reshape(block_count, BLOCK, column_count, BLOCK)
    gate_add = jnp.einsum(
        "aqdh,dhqz->aqz", chosen_entries, gate_segment, preferred_element_type=jnp.float32
    )
    up_increment = jnp.einsum(
        "aqdh,dhqz->aqz", chosen_entries, up_segment, preferred_element_type=jnp.float32
    )
    panel_width = column_count * BLOCK
    hidden = (
        (jax.nn.silu(gate_add) * up_increment).astype(jnp.bfloat16).reshape(rows_here, panel_width)
    )
    column_panel = lax.all_gather(hidden, "tok", axis=0, tiled=True)
    ffn_place = lax.axis_index("ffn")
    begin_col = slab_offset[0] - ffn_place * panel_width
    padded = jnp.pad(hidden, ((0, 0), (SLAB, SLAB)))
    leading_column = jnp.clip(begin_col + SLAB, 0, panel_width + SLAB)
    slab_piece = lax.dynamic_slice_in_dim(padded, leading_column, SLAB, 1).astype(jnp.float32)
    summed = lax.psum(slab_piece.astype(jnp.bfloat16), "ffn")
    row_panel = lax.all_to_all(summed, "tok", split_axis=1, concat_axis=0, tiled=True)
    product = lax.dot_general(
        row_panel, column_panel, (((0,), (0,)), ((), ())), preferred_element_type=jnp.float32
    )
    return product * (2.0 / column_panel.shape[0])


def solution(mesh):
    in_specs = (
        P(("grp", "tok"), "ffn"),
        P(("grp", "tok"), "ffn"),
        P(("grp", "tok"), "ffn"),
        P(("grp", "ffn"), None),
        P("grp"),
    )
    out_specs = P(("grp", "tok"), "ffn")
    return jax.shard_map(shards, mesh=mesh, in_specs=in_specs, out_specs=out_specs, check_vma=False)
```

profile of v0, /device:TPU:0, one launch (start us, length us, event | category | flops | bytes accessed | tf_op | source)
XLA Modules:
  0.0 642.9 jit_solution(3510630286157882670)
XLA Ops:
  6.5 2.3 copy.15
  8.9 0.7 all-gather.7.cloned.1.call-update
  9.6 0.7 all-gather.9.cloned.1.call-update
  10.4 0.7 compare_select_fusion
  11.1 0.1 copy.16
  11.1 0.1 reshape.26
  11.2 0.7 compare_and_fusion
  11.9 0.1 copy.14
  12.7 81.0 %all-gather.5.cloned.1.call-done = bf16[256,16384]{0,1:T(8,128)(2,1)} async-done(((bf16[256,2048]{0,1:T(8,128)(2,1)}), bf16[256,16384]{0,1:T(8,128)(2,1)}) %all-gather.5.cloned.1.call-update) | async-done | bytes 8388624 | tf_op jit(solution)/shard_map/all_gather | solution.py:13
  93.7 12.2 %copy.17 = bf16[256,128,128]{2,0,1:T(8,128)(2,1)} copy(bf16[256,128,128]{0,2,1:T(8,128)(2,1)} %bitcast.44) | data formatting | bytes 16777216 | tf_op jit(solution)/shard_map/reshape | solution.py:14
  106.0 18.3 %gather_fusion = bf16[416,256,128]{2,1,0:T(8,128)(2,1)} fusion(bf16[256,128,128]{2,0,1:T(8,128)(2,1)} %copy.17, s32[1024]{0:T(1024)S(1)} %pad_clamp_fusion), kind=kCustom, calls=%fused_computation | custom fusion | bytes 54527616 | tf_op jit(solution)/shard_map/jit(_take)/gather | solution.py:15
  124.3 101.1 %all-gather.7.cloned.1.call-done = bf16[1024,6656]{1,0:T(8,128)(2,1)} async-done(((bf16[256,6656]{1,0:T(8,128)(2,1)}), bf16[1024,6656]{1,0:T(8,128)(2,1)}) %all-gather.7.cloned.1.call-update) | async-done | bytes 13631504 | tf_op jit(solution)/shard_map/all_gather | solution.py:17
  225.4 22.3 %reshape.36 = bf16[8,128,52,128]{3,2,1,0:T(8,128)(2,1)} reshape(bf16[1024,6656]{1,0:T(8,128)(2,1)} %all-gather.7.cloned.1.call-done) | data formatting | bytes 27262976 | tf_op jit(solution)/shard_map/reshape | solution.py:21
  247.7 19.2 %fusion.2 = f32[52,256,128,1]{1,2,3,0:T(8,128)} fusion(bf16[52,8,256,128]{3,2,1,0:T(8,128)(2,1)} %bitcast.40, pred[52,8]{1,0:T(8,128)(4,1)S(1)} %copy.14, bf16[8,128,52,128]{3,2,1,0:T(8,128)(2,1)} %reshape.36), kind=kOutput, calls=%fused_computation.3 | convolution fusion | flops 3503292416 | bytes 47710624 | tf_op jit(solution)/shard_map/aqdh,dhqz->aqz/dot_general | solution.py:23
  267.0 91.6 %all-gather.9.cloned.1.call-done = bf16[1024,6656]{1,0:T(8,128)(2,1)} async-done(((bf16[256,6656]{1,0:T(8,128)(2,1)}), bf16[1024,6656]{1,0:T(8,128)(2,1)}) %all-gather.9.cloned.1.call-update) | async-done | bytes 13631504 | tf_op jit(solution)/shard_map/all_gather | solution.py:18
  358.5 21.7 %reshape.37 = bf16[8,128,52,128]{3,2,1,0:T(8,128)(2,1)} reshape(bf16[1024,6656]{1,0:T(8,128)(2,1)} %all-gather.9.cloned.1.call-done) | data formatting | bytes 27262976 | tf_op jit(solution)/shard_map/reshape | solution.py:22
  380.3 20.4 %fusion.8 = bf16[256,52,128]{0,2,1:T(8,128)(2,1)S(1)} fusion(f32[52,256,128,1]{1,2,3,0:T(8,128)} %fusion.2, bf16[8,128,52,128]{3,2,1,0:T(8,128)(2,1)} %reshape.37, bf16[52,8,256,128]{3,2,1,0:T(8,128)(2,1)} %bitcast.41, pred[52,8]{1,0:T(8,128)(4,1)S(1)} %copy.14), kind=kOutput, calls=%fused_computation.13 | convolution fusion | flops 3513516032 | bytes 51118496 | tf_op jit(solution)/shard_map/aqdh,dhqz->aqz/dot_general | solution.py:26
  400.7 4.6 pad_dynamic-slice_fusion
  405.4 0.5 all-gather.11.cloned.1.call-update
  405.9 64.5 %all-reduce.3.cloned.1.call-done = bf16[256,4,1024]{0,2,1:T(8,128)(2,1)} async-done(((bf16[256,4,1024]{0,2,1:T(8,128)(2,1)}), bf16[256,4,1024]{0,2,1:T(8,128)(2,1)}) %all-reduce.3.cloned.1.call-update) | async-done | bytes 2097168 | tf_op jit(solution)/shard_map/psum | solution.py:39
  470.4 42.5 %all_to_all.19 = bf16[256,4,1024]{0,2,1:T(8,128)(2,1)S(1)} all-to-all(bf16[256,4,1024]{0,2,1:T(8,128)(2,1)} %all-reduce.3.cloned.1.call-done), channel_id=1, replica_groups=mesh['grp'=1,'ffn'=8,'tok'=4] {'tok'}, dimensions={1} | all-to-all | bytes 4194304 | tf_op jit(solution)/shard_map/all_to_all | solution.py:40
  512.9 2.6 copy.22
  515.4 97.7 %all-gather.11.cloned.1.call-done = bf16[1024,6656]{0,1:T(8,128)(2,1)} async-done(((bf16[256,6656]{0,1:T(8,128)(2,1)}), bf16[1024,6656]{0,1:T(8,128)(2,1)}) %all-gather.11.cloned.1.call-update) | async-done | bytes 13631504 | tf_op jit(solution)/shard_map/all_gather | solution.py:33
  613.1 23.2 %convolution_multiply_fusion = f32[1024,6656]{1,0:T(8,128)} fusion(bf16[1024,1024]{1,0:T(8,128)(2,1)} %bitcast.47, bf16[1024,6656]{0,1:T(8,128)(2,1)} %all-gather.11.cloned.1.call-done), kind=kOutput, calls=%fused_computation.6 | convolution fusion | flops 13965459456 | bytes 42991616 | tf_op jit(solution)/shard_map/dot_general | solution.py:41
  (10 shorter events, 0.2 us)
Async XLA Ops:
  6.5 87.2 %all-gather.5.cloned.1.call-start = ((), (), s32[]{:S(2)}) async-start(), calls=%async_computation.1 | async-start | bytes 9437184 | tf_op jit(solution)/shard_map/all_gather | solution.py:13
  8.8 216.6 %all-gather.7.cloned.1.call-start = ((), (), s32[]{:S(2)}) async-start(), calls=%async_computation.2 | async-start | bytes 17039360 | tf_op jit(solution)/shard_map/all_gather | solution.py:17
  9.6 348.9 %all-gather.9.cloned.1.call-start = ((), (), s32[]{:S(2)}) async-start(), calls=%async_computation.3 | async-start | bytes 17039360 | tf_op jit(solution)/shard_map/all_gather | solution.py:18
  10.3 460.1 %all-reduce.3.cloned.1.call-start = ((), (), s32[]{:S(2)}) async-start(), calls=%async_computation.4 | async-start | bytes 4194304 | tf_op jit(solution)/shard_map/psum | solution.py:39
  400.7 4.7 copy-start
  405.3 207.8 %all-gather.11.cloned.1.call-start = ((), (), s32[]{:S(2)}) async-start(), calls=%async_computation.5 | async-start | bytes 17039360 | tf_op jit(solution)/shard_map/all_gather | solution.py:33
Sparse Core Ops, SparseCore 0:
  9.0 84.7 all-gather.4
  95.6 129.7 all-gather.6
  227.2 131.2 all-gather.8
  405.5 64.9 all-reduce.2
  472.1 141.0 all-gather.10
where the time goes:
time: 645 us; the launch traced here: 643 us
  waiting for transfers between devices  438 us (68%)
  local copies, waits for them, and re-layouts  84.4 us (13%)
  matrix products  62.9 us (10%)
  blocking collectives  42.5 us (7%)
  between operations  13.8 us (2%)
    all_gather x1, waiting for transfers between devices, shards(): lax.all_gather(gate_blocks, 'tok', axis=0, tiled=True)  101 us
    all_gather x1, waiting for transfers between devices, shards(): column_panel = lax.all_gather(hidden, 'tok', axis=0, tiled=True)  97.7 us
    all_gather x1, waiting for transfers between devices, shards(): lax.all_gather(up_blocks, 'tok', axis=0, tiled=True)  91.6 us
    all_gather x1, waiting for transfers between devices, shards(): whole = lax.all_gather(tokens, 'ffn', axis=1, tiled=True)  81 us
    psum x1, waiting for transfers between devices, shards(): summed = lax.psum(slab_piece.astype(jnp.bfloat16), 'ffn')  64.5 us
    all_to_all x1, blocking collectives, shards(): lax.all_to_all(summed, 'tok', split_axis=1, concat_axis=0, tiled=True)  42.5 us
    dot_general x1, matrix products, shards(): lax.dot_general(row_panel, column_panel, (((0,), (0,)), ((), ())), prefer...  23.2 us
    reshape x1, local copies, waits for them, and re-layouts, shards(): gate_segment = pieces[0].reshape(block_count, BLOCK, column_count, BLOCK)  22.3 us
  transfers between devices with their start and end apart: 5, of which 5 were waited for; matrix products, arithmetic and copies ran while one was open for 12% of the time, Pallas kernels for 0%

commit v1 on v0

--- a/solution.py
+++ b/solution.py
@@ -1,10 +1,276 @@
+import functools
+
 import jax
 import jax.numpy as jnp
 from jax import lax
+from jax.experimental import pallas as pl
+from jax.experimental.pallas import tpu as pltpu
 from jax.sharding import PartitionSpec as P
 
 BLOCK = 128
 SLAB = 4096
+MESH = pl.DeviceIdType.MESH
+ANY = pl.BlockSpec(memory_space=pl.ANY)
+
+
+def remote(src, dst, send, recv, **where):
+    return pltpu.make_async_remote_copy(
+        src_ref=src, dst_ref=dst, send_sem=send, recv_sem=recv, device_id=where, device_id_type=MESH
+    )
+
+
+def greet(others, z_there):
+    barrier = pltpu.get_barrier_semaphore()
+    for where in others:
+        pl.semaphore_signal(barrier, inc=1, device_id=where, device_id_type=MESH)
+    for there, where in z_there:
+        @pl.when(there)
+        def _():
+            pl.semaphore_signal(barrier, inc=1, device_id=where, device_id_type=MESH)
+    count = len(others)
+    for there, _ in z_there:
+        count = count + jnp.where(there, 1, 0)
+    pl.semaphore_wait(barrier, count)
+
+
+def places():
+    f, t = lax.axis_index("ffn"), lax.axis_index("tok")
+    z, c = f // 2, f % 2
+    y, x = t // 2, t % 2
+    return f, t, z, c, y, x
+
+
+def spread(chips, tok_ref, gate_ref, up_ref, t_ref, g_ref, u_ref,
+           w_send, w_recv, l_sem, x_send, x_recv, c_send, c_recv, up_send, up_recv, dn_send, dn_recv):
+    f, t, z, c, y, x = places()
+    half = g_ref.shape[2]
+    xn, yn, dn = y * 2 + 1 - x, (1 - y) * 2 + x, (1 - y) * 2 + 1 - x
+    partner = z * 2 + 1 - c
+    above, below = f + 2, f - 2
+    greet(
+        [dict(tok=xn), dict(tok=yn), dict(tok=dn), dict(ffn=partner)],
+        [(z < chips - 1, dict(ffn=above)), (z > 0, dict(ffn=below))],
+    )
+    ends = []
+    own = t_ref.at[f, x]
+    cx = remote(tok_ref, own, x_send, x_recv, tok=xn)
+    cx.start()
+
+    def up(src, dst, zs, j):
+        return remote(src, dst, up_send.at[zs, j], up_recv.at[zs, j], ffn=above)
+
+    def down(src, dst, zs, j):
+        return remote(src, dst, dn_send.at[zs, j], dn_recv.at[zs, j], ffn=below)
+
+    def across(src, dst, zs, j):
+        return remote(src, dst, c_send.at[zs, j], c_recv.at[zs, j], ffn=partner)
+
+    def pass_on(src, dst, zs, j, go_up, go_down):
+        if go_up is not None:
+            @pl.when(go_up)
+            def _():
+                up(src, dst, zs, j).start()
+        if go_down is not None:
+            @pl.when(go_down)
+            def _():
+                down(src, dst, zs, j).start()
+        across(src, dst, zs, j).start()
+
+    pass_on(tok_ref, own, z, 0, z < chips - 1, z > 0)
+    copies = []
+    for k, (there, x_there) in enumerate(((xn, 1 - x), (yn, x), (dn, 1 - x))):
+        cols = pl.ds(pl.multiple_of(x_there * half, BLOCK), half)
+        for m, (src, dst) in enumerate(((gate_ref, g_ref), (up_ref, u_ref))):
+            copy = remote(src.at[:, cols], dst.at[t], w_send.at[k, m], w_recv.at[k, m], tok=there)
+            copy.start()
+            copies.append(copy)
+    cols = pl.ds(pl.multiple_of(x * half, BLOCK), half)
+    locals_ = [
+        pltpu.make_async_copy(tok_ref, own, l_sem.at[0]),
+        pltpu.make_async_copy(gate_ref.at[:, cols], g_ref.at[t], l_sem.at[1]),
+        pltpu.make_async_copy(up_ref.at[:, cols], u_ref.at[t], l_sem.at[2]),
+    ]
+    for copy in locals_:
+        copy.start()
+    other = t_ref.at[f, 1 - x]
+    remote(tok_ref, other, x_send, x_recv, tok=xn).wait_recv()
+    pass_on(other, other, z, 1, z < chips - 1, z > 0)
+    for k in range(1, chips):
+        for j in range(2):
+            xs = x if j == 0 else 1 - x
+
+            @pl.when(z >= k)
+            def _():
+                piece = t_ref.at[f - 2 * k, xs]
+                up(piece, piece, z - k, j).wait_recv()
+                pass_on(piece, piece, z - k, j, z < chips - 1, None)
+
+            @pl.when(z + k < chips)
+            def _():
+                piece = t_ref.at[f + 2 * k, xs]
+                down(piece, piece, z + k, j).wait_recv()
+                pass_on(piece, piece, z + k, j, None, z > 0)
+
+    for zs in range(chips):
+        for j in range(2):
+            xs = x if j == 0 else 1 - x
+            got = t_ref.at[zs * 2 + 1 - c, xs]
+            across(got, got, zs, j).wait_recv()
+            across(got, got, zs, j).wait_send()
+
+            @pl.when((zs <= z) & (z < chips - 1))
+            def _():
+                up(got, got, zs, j).wait_send()
+
+            @pl.when((zs >= z) & (z > 0))
+            def _():
+                down(got, got, zs, j).wait_send()
+
+    cx.wait_send()
+    for copy in locals_:
+        copy.wait()
+    for copy in copies:
+        copy.wait()
+
+
+def join(h_ref, p_ref, l_sem, send, recv):
+    f, t, z, c, y, x = places()
+    rows, half = h_ref.shape
+    xn, yn, dn = y * 2 + 1 - x, (1 - y) * 2 + x, (1 - y) * 2 + 1 - x
+    greet([dict(tok=xn), dict(tok=yn)], [])
+    cut = rows // 2
+
+    def part(yy, xx, s):
+        return p_ref.at[
+            pl.ds(pl.multiple_of(yy * rows + s * cut, 16), cut),
+            pl.ds(pl.multiple_of(xx * half, BLOCK), half),
+        ]
+
+    local = pltpu.make_async_copy(
+        h_ref,
+        p_ref.at[pl.ds(pl.multiple_of(y * rows, 16), rows), pl.ds(pl.multiple_of(x * half, BLOCK), half)],
+        l_sem,
+    )
+
+    def copy(src, yy, xx, s, n, there):
+        return remote(src, part(yy, xx, s), send.at[n], recv.at[n], tok=there)
+
+    own = [h_ref.at[pl.ds(s * cut, cut)] for s in range(2)]
+    sent = [
+        copy(own[0], y, x, 0, 0, xn), copy(own[1], y, x, 1, 2, yn),
+        copy(own[1], y, x, 1, 1, xn), copy(own[0], y, x, 0, 3, yn),
+    ]
+    for s in sent:
+        s.start()
+    local.start()
+    a = part(y, 1 - x, 0)
+    copy(a, y, 1 - x, 0, 0, xn).wait_recv()
+    fy = copy(a, y, 1 - x, 0, 4, yn)
+    fy.start()
+    b = part(1 - y, x, 1)
+    copy(b, 1 - y, x, 1, 2, yn).wait_recv()
+    fx = copy(b, 1 - y, x, 1, 5, xn)
+    fx.start()
+    sent[2].wait_recv()
+    sent[3].wait_recv()
+    fy.wait()
+    fx.wait()
+    for s in sent:
+        s.wait_send()
+    local.wait()
+
+
+def hidden_kernel(per, rows_ref, t_ref, g_ref, u_ref, h_ref):
+    i = pl.program_id(0)
+    depth = g_ref.shape[0]
+    tiles = []
+    for k in range(depth // BLOCK):
+        r = rows_ref[i, k]
+        tile = t_ref[r // per, :, :, pl.ds(pl.multiple_of((r % per) * BLOCK, BLOCK), BLOCK)]
+        tiles.append(tile.reshape(-1, BLOCK))
+    picked = jnp.concatenate(tiles, axis=1)
+    weights = jnp.concatenate([g_ref[...], u_ref[...]], axis=1)
+    both = jnp.dot(picked, weights, preferred_element_type=jnp.float32)
+    gate, up = both[:, :BLOCK], both[:, BLOCK:]
+    h_ref[...] = (gate / (1.0 + jnp.exp(-gate)) * up).astype(h_ref.dtype)
+
+
+def product_kernel(scale, a_ref, b_ref, o_ref):
+    o_ref[...] = jnp.dot(a_ref[...], b_ref[...], preferred_element_type=jnp.float32) * scale
+
+
+def params(**more):
+    return pltpu.CompilerParams(**more)
+
+
+def shards_split(ffn, tokens, gate_blocks, up_blocks, block_rows, slab_offset):
+    rows, feats = tokens.shape
+    depth, panel = gate_blocks.shape
+    half = panel // 2
+    chips = ffn // 2
+    bf = jnp.bfloat16
+    dma = pltpu.SemaphoreType.DMA
+    shape = jax.ShapeDtypeStruct
+    spread_tokens, gates, ups = pl.pallas_call(
+        functools.partial(spread, chips),
+        out_shape=(shape((ffn, 2, rows, feats), bf), shape((4, depth, half), bf), shape((4, depth, half), bf)),
+        in_specs=[ANY] * 3,
+        out_specs=(ANY,) * 3,
+        scratch_shapes=[
+            dma((3, 2)), dma((3, 2)), dma((3,)), dma, dma,
+            dma((chips, 2)), dma((chips, 2)), dma((chips, 2)),
+            dma((chips, 2)), dma((chips, 2)), dma((chips, 2)),
+        ],
+        compiler_params=params(collective_id=0, has_side_effects=True),
+        name="spread",
+    )(tokens, gate_blocks, up_blocks)
+    t = lax.axis_index("tok")
+    f = lax.axis_index("ffn")
+    count = half // BLOCK
+    rows_here = lax.dynamic_slice_in_dim(block_rows, (t % 2) * count, count, 0)
+    hidden = pl.pallas_call(
+        functools.partial(hidden_kernel, feats // BLOCK),
+        out_shape=shape((2 * rows, half), bf),
+        grid_spec=pltpu.PrefetchScalarGridSpec(
+            num_scalar_prefetch=1,
+            grid=(count,),
+            in_specs=[
+                pl.BlockSpec(memory_space=pltpu.VMEM),
+                pl.BlockSpec((4 * depth, BLOCK), lambda i, r: (0, i)),
+                pl.BlockSpec((4 * depth, BLOCK), lambda i, r: (0, i)),
+            ],
+            out_specs=pl.BlockSpec((2 * rows, BLOCK), lambda i, r: (0, i)),
+        ),
+        compiler_params=params(vmem_limit_bytes=48 * 1024 * 1024),
+        name="hidden",
+    )(rows_here, spread_tokens, gates.reshape(4 * depth, half), ups.reshape(4 * depth, half))
+    whole = pl.pallas_call(
+        join,
+        out_shape=shape((4 * rows, panel), bf),
+        in_specs=[ANY],
+        out_specs=ANY,
+        scratch_shapes=[dma, dma((6,)), dma((6,))],
+        compiler_params=params(collective_id=1, has_side_effects=True),
+        name="join",
+    )(hidden)
+    wide = SLAB // 4
+    begin = slab_offset[0] + t * wide - f * panel
+    padded = jnp.pad(whole, ((0, 0), (wide, wide)))
+    piece = lax.dynamic_slice_in_dim(padded, jnp.clip(begin + wide, 0, panel + wide), wide, 1)
+    row_panel = lax.psum(piece, "ffn").T
+    tile = 512 if panel % 512 == 0 else BLOCK
+    return pl.pallas_call(
+        functools.partial(product_kernel, 2.0 / (4 * rows)),
+        out_shape=shape((wide, panel), jnp.float32),
+        grid=(panel // tile,),
+        in_specs=[
+            pl.BlockSpec((wide, 4 * rows), lambda i: (0, 0)),
+            pl.BlockSpec((4 * rows, tile), lambda i: (0, i)),
+        ],
+        out_specs=pl.BlockSpec((wide, tile), lambda i: (0, i)),
+        compiler_params=params(vmem_limit_bytes=48 * 1024 * 1024),
+        name="product",
+    )(row_panel, whole)
 
 
 def shards(tokens, gate_blocks, up_blocks, block_rows, slab_offset):
@@ -45,6 +311,13 @@
 
 
 def solution(mesh):
+    ffn, tok = mesh.shape["ffn"], mesh.shape["tok"]
+
+    def body(tokens, gate_blocks, up_blocks, block_rows, slab_offset):
+        if tok == 4 and ffn % 2 == 0 and block_rows.shape[0] % 2 == 0:
+            return shards_split(ffn, tokens, gate_blocks, up_blocks, block_rows, slab_offset)
+        return shards(tokens, gate_blocks, up_blocks, block_rows, slab_offset)
+
     in_specs = (
         P(("grp", "tok"), "ffn"),
         P(("grp", "tok"), "ffn"),
@@ -53,4 +326,4 @@
         P("grp"),
     )
     out_specs = P(("grp", "tok"), "ffn")
-    return jax.shard_map(shards, mesh=mesh, in_specs=in_specs, out_specs=out_specs, check_vma=False)
+    return jax.shard_map(body, mesh=mesh, in_specs=in_specs, out_specs=out_specs, check_vma=False)

time: 645 us -> 443 us (0.69)
  waiting for transfers between devices: 438 us -> 65.9 us
  Pallas kernels: 0 us -> 337 us
  matrix products: 62.9 us -> 0 us
  local copies, waits for them, and re-layouts: 84.4 us -> 24.3 us
  blocking collectives: 42.5 us -> 0 us
    all_gather x4 -> x0, waiting for transfers between devices: 371 us -> none  [the longest x1 101 us: shards(): lax.all_gather(gate_blocks, 'tok', axis=0, tiled=True)]
    pallas_call x0 -> x4, Pallas kernels: none -> 337 us  [the longest x1 175 us: shards_split(): pl.pallas_call(functools.partial(spread, chips), out_shape=(shape((ffn, 2...]
    dot_general x3 -> x0, matrix products: 62.9 us -> none  [the longest x1 23.2 us: shards(): lax.dot_general(row_panel, column_panel, (((0,), (0,)), ((), ())), prefer...]
    reshape x3 -> x0, local copies, waits for them, and re-layouts: 56.3 us -> none  [the longest x1 22.3 us: shards(): gate_segment = pieces[0].reshape(block_count, BLOCK, column_count, BLOCK)]
    all_to_all x1 -> x0, blocking collectives: 42.5 us -> none  [shards(): lax.all_to_all(summed, 'tok', split_axis=1, concat_axis=0, tiled=True)]
    pallas_call x0 -> x1, local copies, waits for them, and re-layouts: none -> 18.4 us  [shards_split(): pl.pallas_call(join, out_shape=shape((4 * rows, panel), bf), in_specs=[AN...]
    gather x1 -> x0, local copies, waits for them, and re-layouts: 18.3 us -> none  [shards(): chosen_entries = jnp.take(feature_tiles, block_rows, axis=1)]
  transfers between devices with their start and end apart: 5 -> 1, of which waited for: 5 -> 1; matrix products, arithmetic and copies ran while one was open for 12% -> 0% of each run, Pallas kernels for 0% -> 0%
where the time goes in v1:
time: 443 us; the launch traced here: 441 us
  Pallas kernels  337 us (76%)
  waiting for transfers between devices  65.9 us (15%)
  local copies, waits for them, and re-layouts  24.3 us (5%)
  between operations  14.1 us (3%)
    pallas_call x1, Pallas kernels, shards_split(): pl.pallas_call(functools.partial(spread, chips), out_shape=(shape((ffn, 2...  175 us
    pallas_call x1, Pallas kernels, shards_split(): pl.pallas_call(join, out_shape=shape((4 * rows, panel), bf), in_specs=[AN...  112 us
    psum x1, waiting for transfers between devices, shards_split(): row_panel = lax.psum(piece, 'ffn').T  65.9 us
    pallas_call x1, Pallas kernels, shards_split(): pl.pallas_call(functools.partial(hidden_kernel, feats // BLOCK), out_shap...  26.5 us
    pallas_call x1, Pallas kernels, shards_split(): pl.pallas_call(functools.partial(product_kernel, 2.0 / (4 * rows)), out_s...  23.5 us
    pallas_call x1, local copies, waits for them, and re-layouts, shards_split(): pl.pallas_call(join, out_shape=shape((4 * rows, panel), bf), in_specs=[AN...  18.4 us
  transfers between devices with their start and end apart: 1, of which 1 were waited for; matrix products, arithmetic and copies ran while one was open for 0% of the time, Pallas kernels for 0%

profile of v1, /device:TPU:0, one launch (start us, length us, event | category | flops | bytes accessed | tf_op | source)
XLA Modules:
  0.0 441.1 jit_solution(8722360544738529846)
XLA Ops:
  6.5 0.0 copy-start
  6.5 0.0 all-reduce.3.cloned.1.call-start
  7.2 0.0 copy-done
  7.2 0.1 constant_dynamic-slice_fusion
  7.3 0.1 copy.8.rows_ref
  7.4 175.3 %spread.1 = (bf16[8,2,256,2048]{3,2,1,0:T(8,128)(2,1)}, bf16[4,256,3328]{2,1,0:T(8,128)(2,1)}, bf16[4,256,3328]{2,1,0:T(8,128)(2,1)}) custom-call(bf16[256,2048]{1,0:T(8,128)(2,1)} %tok_ref.1, bf16[256,6656]{1,0:T(8,128)(2,1)} %gate_ref.1, bf16[256,6656]{1,0:T(8,128)(2,1)} %up_ref.1), custom_call_target="tpu_custom_call" | custom-call | tf_op jit(solution)/shard_map/spread/pallas_call | solution.py:214
  182.7 26.5 %hidden.1.h_ref = bf16[512,3328]{1,0:T(8,128)(2,1)S(1)} custom-call(s32[26,8]{1,0:T(8,128)S(1)} %copy.8.rows_ref, bf16[8,2,256,2048]{3,2,1,0:T(8,128)(2,1)} %get-tuple-element.8.t_ref, bf16[1024,3328]{1,0:T(8,128)(2,1)} %bitcast.6, bf16[1024,3328]{1,0:T(8,128)(2,1)} %bitcast.7), custom_call_target="tpu_custom_call" | custom-call | tf_op jit(solution)/shard_map/hidden/pallas_call | solution.py:231
  209.2 0.0 copy-start.2
  209.2 1.7 copy-done.2
  210.9 111.5 %join.1.b_ref = bf16[1024,6656]{1,0:T(8,128)(2,1)} custom-call(bf16[512,3328]{1,0:T(8,128)(2,1)} %copy-done.2), custom_call_target="tpu_custom_call" | custom-call | tf_op jit(solution)/shard_map/join/pallas_call | solution.py:247
  322.5 18.4 %copy.7 = bf16[1024,6656]{0,1:T(8,128)(2,1)} copy(bf16[1024,6656]{1,0:T(8,128)(2,1)} %join.1.b_ref) | data formatting | bytes 27262976 | tf_op jit(solution)/shard_map/join/pallas_call | solution.py:247
  340.9 2.4 fusion
  343.2 0.0 all-reduce.3.cloned.1.call-update
  343.3 65.9 %all-reduce.3.cloned.1.call-done.a_ref = bf16[1024,1024]{1,0:T(8,128)(2,1)} async-done(((bf16[1024,1024]{1,0:T(8,128)(2,1)}), bf16[1024,1024]{1,0:T(8,128)(2,1)}) %all-reduce.3.cloned.1.call-update) | async-done | bytes 2097168 | tf_op jit(solution)/shard_map/psum | solution.py:260
  409.2 0.0 copy-start.3
  409.2 1.6 copy-done.3
  410.7 0.0 copy-start.1
  410.7 23.5 %product.1 = f32[1024,6656]{1,0:T(8,128)} custom-call(bf16[1024,1024]{1,0:T(8,128)(2,1)S(1)} %copy-done.3, bf16[1024,6656]{1,0:T(8,128)(2,1)} %join.1.b_ref), custom_call_target="tpu_custom_call" | custom-call | tf_op jit(solution)/shard_map/product/pallas_call | solution.py:262
  434.3 0.0 copy-done.1
Async XLA Ops:
  6.5 0.7 copy-start
  6.5 402.6 %all-reduce.3.cloned.1.call-start = ((), (), s32[]{:S(2)}) async-start(), calls=%async_computation | async-start | bytes 4194304 | tf_op jit(solution)/shard_map/psum | solution.py:260
  209.2 1.8 copy-start.2
  409.2 1.6 copy-start.3
  410.7 23.5 %copy-start.1 = (s32[52,8]{0,1:T(8,128)S(1)}, s32[52,8]{0,1:T(8,128)}, u32[]{:S(2)}) copy-start(s32[52,8]{0,1:T(8,128)} %param.8) | copy-start | bytes 4996
Sparse Core Ops, SparseCore 0:
  343.4 65.7 all-reduce.2

commit v2 on v1

--- a/solution.py
+++ b/solution.py
@@ -133,11 +133,21 @@
         copy.wait()
 
 
-def join(h_ref, p_ref, l_sem, send, recv):
+CHUNKS = 4
+
+
+def join(chips, h_ref, s_ref, p_ref, r_ref, a, b, d, e, pin, qin, pout, qout,
+         l_sem, send, recv, b_sem, d_send, d_recv, p_send, p_recv, q_send, q_recv, r_send, r_recv):
     f, t, z, c, y, x = places()
     rows, half = h_ref.shape
-    xn, yn, dn = y * 2 + 1 - x, (1 - y) * 2 + x, (1 - y) * 2 + 1 - x
-    greet([dict(tok=xn), dict(tok=yn)], [])
+    xn, yn = y * 2 + 1 - x, (1 - y) * 2 + x
+    partner = z * 2 + 1 - c
+    above, below = f + 2, f - 2
+    has_up, has_down = z < chips - 1, z > 0
+    greet(
+        [dict(tok=xn), dict(tok=yn), dict(ffn=partner)],
+        [(has_up, dict(ffn=above)), (has_down, dict(ffn=below))],
+    )
     cut = rows // 2
 
     def part(yy, xx, s):
@@ -146,12 +156,6 @@
             pl.ds(pl.multiple_of(xx * half, BLOCK), half),
         ]
 
-    local = pltpu.make_async_copy(
-        h_ref,
-        p_ref.at[pl.ds(pl.multiple_of(y * rows, 16), rows), pl.ds(pl.multiple_of(x * half, BLOCK), half)],
-        l_sem,
-    )
-
     def copy(src, yy, xx, s, n, there):
         return remote(src, part(yy, xx, s), send.at[n], recv.at[n], tok=there)
 
@@ -160,17 +164,137 @@
         copy(own[0], y, x, 0, 0, xn), copy(own[1], y, x, 1, 2, yn),
         copy(own[1], y, x, 1, 1, xn), copy(own[0], y, x, 0, 3, yn),
     ]
-    for s in sent:
-        s.start()
+    mine, theirs = (pl.ds(pl.multiple_of(k * cut, 16), cut) for k in (c, 1 - c))
+    swap = remote(s_ref.at[:, theirs], b, b_sem.at[0], b_sem.at[1], ffn=partner)
+    swap.start()
+    load = pltpu.make_async_copy(s_ref.at[:, mine], a, l_sem.at[1])
+    load.start()
+    sent[0].start()
+    sent[1].start()
+    sent[3].start()
+    local = pltpu.make_async_copy(
+        h_ref,
+        p_ref.at[pl.ds(pl.multiple_of(y * rows, 16), rows), pl.ds(pl.multiple_of(x * half, BLOCK), half)],
+        l_sem.at[0],
+    )
     local.start()
-    a = part(y, 1 - x, 0)
-    copy(a, y, 1 - x, 0, 0, xn).wait_recv()
-    fy = copy(a, y, 1 - x, 0, 4, yn)
+    load.wait()
+    swap.wait()
+
+    strip = cut // CHUNKS
+
+    def strip_of(k):
+        return pl.ds(pl.multiple_of(k * strip, 16), strip)
+
+    @pl.loop(0, CHUNKS)
+    def _(k):
+        a[:, strip_of(k)] = a[:, strip_of(k)] + b[:, strip_of(k)]
+
+    over = [
+        remote(a.at[yy * 2 + 1 - x], d.at[yy], d_send.at[yy], d_recv.at[yy], tok=xn) for yy in range(2)
+    ]
+    for o in over:
+        o.start()
+    for o in over:
+        o.wait()
+    sent[2].start()
+
+    @pl.loop(0, CHUNKS)
+    def _(k):
+        for yy in range(2):
+            e[yy, strip_of(k)] = a[yy * 2 + x, strip_of(k)] + d[yy, strip_of(k)]
+
+    def rise(k):
+        return remote(pout.at[:, strip_of(k)], pin.at[:, strip_of(k)], p_send.at[k], p_recv.at[k], ffn=above)
+
+    def fall(k):
+        return remote(qout.at[:, strip_of(k)], qin.at[:, strip_of(k)], q_send.at[k], q_recv.at[k], ffn=below)
+
+    def line(first, last):
+        for step in range(first, last):
+            k = step - z
+
+            @pl.when((k >= 0) & (k < CHUNKS))
+            def _():
+                @pl.when(z == 0)
+                def _():
+                    pout[:, strip_of(k)] = e[:, strip_of(k)]
+
+                @pl.when(has_down)
+                def _():
+                    rise(k).wait_recv()
+                    pout[:, strip_of(k)] = e[:, strip_of(k)] + pin[:, strip_of(k)]
+
+                @pl.when(has_up)
+                def _():
+                    rise(k).start()
+
+            n = step - (chips - 1 - z)
+
+            @pl.when((n >= 0) & (n < CHUNKS))
+            def _():
+                @pl.when(z == chips - 1)
+                def _():
+                    qout[:, strip_of(n)] = e[:, strip_of(n)]
+
+                @pl.when(has_up)
+                def _():
+                    fall(n).wait_recv()
+                    qout[:, strip_of(n)] = e[:, strip_of(n)] + qin[:, strip_of(n)]
+
+                @pl.when(has_down)
+                def _():
+                    fall(n).start()
+
+    line(0, 2)
+    via_x = part(y, 1 - x, 0)
+    copy(via_x, y, 1 - x, 0, 0, xn).wait_recv()
+    fy = copy(via_x, y, 1 - x, 0, 4, yn)
     fy.start()
-    b = part(1 - y, x, 1)
-    copy(b, 1 - y, x, 1, 2, yn).wait_recv()
-    fx = copy(b, 1 - y, x, 1, 5, xn)
+    line(2, CHUNKS + chips - 1)
+
+    @pl.loop(0, CHUNKS)
+    def _(k):
+        @pl.when(has_up)
+        def _():
+            e[:, strip_of(k)] = pout[:, strip_of(k)] + qin[:, strip_of(k)]
+
+        @pl.when(z == chips - 1)
+        def _():
+            e[:, strip_of(k)] = pout[:, strip_of(k)]
+
+    def slab_rows(yy):
+        return r_ref.at[pl.ds(pl.multiple_of(yy * rows + c * cut, 16), cut)]
+
+    to_y = remote(e.at[1 - y], slab_rows(y), r_send.at[0], r_recv.at[0], tok=yn)
+    to_y.start()
+    to_core = remote(e.at[y], slab_rows(y), r_send.at[1], r_recv.at[1], ffn=partner)
+    to_core.start()
+    keep = pltpu.make_async_copy(e.at[y], slab_rows(y), l_sem.at[2])
+    keep.start()
+    via_y = part(1 - y, x, 1)
+    copy(via_y, 1 - y, x, 1, 2, yn).wait_recv()
+    fx = copy(via_y, 1 - y, x, 1, 5, xn)
     fx.start()
+    from_y = slab_rows(1 - y)
+    remote(e.at[1 - y], from_y, r_send.at[0], r_recv.at[0], tok=yn).wait_recv()
+    again = remote(from_y, from_y, r_send.at[2], r_recv.at[2], ffn=partner)
+    again.start()
+    to_y.wait_send()
+    to_core.wait()
+    keep.wait()
+    again.wait()
+
+    @pl.loop(0, CHUNKS)
+    def _(k):
+        @pl.when(has_up)
+        def _():
+            rise(k).wait_send()
+
+        @pl.when(has_down)
+        def _():
+            fall(k).wait_send()
+
     sent[2].wait_recv()
     sent[3].wait_recv()
     fy.wait()
@@ -180,7 +304,7 @@
     local.wait()
 
 
-def hidden_kernel(per, rows_ref, t_ref, g_ref, u_ref, h_ref):
+def hidden_kernel(per, rows_ref, begin_ref, t_ref, g_ref, u_ref, h_ref, s_ref):
     i = pl.program_id(0)
     depth = g_ref.shape[0]
     tiles = []
@@ -192,7 +316,19 @@
     weights = jnp.concatenate([g_ref[...], u_ref[...]], axis=1)
     both = jnp.dot(picked, weights, preferred_element_type=jnp.float32)
     gate, up = both[:, :BLOCK], both[:, BLOCK:]
-    h_ref[...] = (gate / (1.0 + jnp.exp(-gate)) * up).astype(h_ref.dtype)
+    hidden = (gate / (1.0 + jnp.exp(-gate)) * up).astype(h_ref.dtype)
+    h_ref[...] = hidden
+
+    @pl.when(i == 0)
+    def _():
+        s_ref[...] = jnp.zeros_like(s_ref)
+
+    wide = s_ref.shape[2] // BLOCK
+    at = i - begin_ref[0]
+
+    @pl.when((at >= 0) & (at < wide * s_ref.shape[0]))
+    def _():
+        s_ref[at // wide, :, pl.ds(pl.multiple_of((at % wide) * BLOCK, BLOCK), BLOCK)] = hidden
 
 
 def product_kernel(scale, a_ref, b_ref, o_ref):
@@ -228,36 +364,46 @@
     f = lax.axis_index("ffn")
     count = half // BLOCK
     rows_here = lax.dynamic_slice_in_dim(block_rows, (t % 2) * count, count, 0)
-    hidden = pl.pallas_call(
+    wide = SLAB // 4
+    begin = slab_offset // BLOCK - (f * 2 + t % 2) * count
+    hidden, slab = pl.pallas_call(
         functools.partial(hidden_kernel, feats // BLOCK),
-        out_shape=shape((2 * rows, half), bf),
+        out_shape=(shape((2 * rows, half), bf), shape((4, 2 * rows, wide), bf)),
         grid_spec=pltpu.PrefetchScalarGridSpec(
-            num_scalar_prefetch=1,
+            num_scalar_prefetch=2,
             grid=(count,),
             in_specs=[
                 pl.BlockSpec(memory_space=pltpu.VMEM),
-                pl.BlockSpec((4 * depth, BLOCK), lambda i, r: (0, i)),
-                pl.BlockSpec((4 * depth, BLOCK), lambda i, r: (0, i)),
+                pl.BlockSpec((4 * depth, BLOCK), lambda i, r, b: (0, i)),
+                pl.BlockSpec((4 * depth, BLOCK), lambda i, r, b: (0, i)),
             ],
-            out_specs=pl.BlockSpec((2 * rows, BLOCK), lambda i, r: (0, i)),
+            out_specs=(
+                pl.BlockSpec((2 * rows, BLOCK), lambda i, r, b: (0, i)),
+                pl.BlockSpec((4, 2 * rows, wide), lambda i, r, b: (0, 0, 0)),
+            ),
         ),
         compiler_params=params(vmem_limit_bytes=48 * 1024 * 1024),
         name="hidden",
-    )(rows_here, spread_tokens, gates.reshape(4 * depth, half), ups.reshape(4 * depth, half))
-    whole = pl.pallas_call(
-        join,
-        out_shape=shape((4 * rows, panel), bf),
-        in_specs=[ANY],
-        out_specs=ANY,
-        scratch_shapes=[dma, dma((6,)), dma((6,))],
-        compiler_params=params(collective_id=1, has_side_effects=True),
+    )(rows_here, begin, spread_tokens, gates.reshape(4 * depth, half), ups.reshape(4 * depth, half))
+    vmem = pltpu.VMEM
+    whole, row_panel = pl.pallas_call(
+        functools.partial(join, chips),
+        out_shape=(shape((4 * rows, panel), bf), shape((4 * rows, wide), bf)),
+        in_specs=[ANY] * 2,
+        out_specs=(ANY,) * 2,
+        scratch_shapes=[
+            vmem((4, rows, wide), bf), vmem((4, rows, wide), bf),
+            *[vmem((2, rows, wide), bf) for _ in range(6)],
+            dma((3,)), dma((6,)), dma((6,)), dma((2,)), dma((2,)), dma((2,)),
+            *[dma((CHUNKS,)) for _ in range(4)],
+            dma((3,)), dma((3,)),
+        ],
+        compiler_params=params(
+            collective_id=1, has_side_effects=True, vmem_limit_bytes=32 * 1024 * 1024
+        ),
         name="join",
-    )(hidden)
-    wide = SLAB // 4
-    begin = slab_offset[0] + t * wide - f * panel
-    padded = jnp.pad(whole, ((0, 0), (wide, wide)))
-    piece = lax.dynamic_slice_in_dim(padded, jnp.clip(begin + wide, 0, panel + wide), wide, 1)
-    row_panel = lax.psum(piece, "ffn").T
+    )(hidden, slab)
+    row_panel = row_panel.T
     tile = 512 if panel % 512 == 0 else BLOCK
     return pl.pallas_call(
         functools.partial(product_kernel, 2.0 / (4 * rows)),

time: 443 us -> 375 us (0.85)
  waiting for transfers between devices: 65.9 us -> 0 us
  Pallas kernels: 337 us -> 367 us
  local copies, waits for them, and re-layouts: 24.3 us -> 6.53 us
  between operations: 14.1 us -> 0.74 us
    psum x1 -> x0, waiting for transfers between devices: 65.9 us -> none  [shards_split(): row_panel = lax.psum(piece, 'ffn').T]
    pallas_call x1, Pallas kernels: 112 us -> 139 us  [shards_split(): pl.pallas_call(functools.partial(join, chips), out_shape=(shape((4 * rows...]
    pallas_call x1, local copies, waits for them, and re-layouts: 18.4 us -> 2.85 us  [shards_split(): pl.pallas_call(functools.partial(join, chips), out_shape=(shape((4 * rows...]
  transfers between devices with their start and end apart: 1 -> 0, of which waited for: 1 -> 0; matrix products, arithmetic and copies ran while one was open for 0% -> 0% of each run, Pallas kernels for 0% -> 0%
where the time goes in v2:
time: 375 us; the launch traced here: 374 us
  Pallas kernels  367 us (98%)
  local copies, waits for them, and re-layouts  6.53 us (2%)
    pallas_call x1, Pallas kernels, shards_split(): pl.pallas_call(functools.partial(spread, chips), out_shape=(shape((ffn, 2...  175 us
    pallas_call x1, Pallas kernels, shards_split(): pl.pallas_call(functools.partial(join, chips), out_shape=(shape((4 * rows...  139 us
    pallas_call x1, Pallas kernels, shards_split(): pl.pallas_call(functools.partial(hidden_kernel, feats // BLOCK), out_shap...  29.1 us
    pallas_call x1, Pallas kernels, shards_split(): pl.pallas_call(functools.partial(product_kernel, 2.0 / (4 * rows)), out_s...  23.5 us

profile of v2, /device:TPU:0, one launch (start us, length us, event | category | flops | bytes accessed | tf_op | source)
XLA Modules:
  0.0 373.9 jit_solution(13996631868240943518)
XLA Ops:
  0.0 0.0 copy-start
  0.7 0.0 copy-done
  0.7 0.1 constant_dynamic-slice_fusion
  0.8 0.1 copy.8.rows_ref
  0.9 175.3 %spread.1 = (bf16[8,2,256,2048]{3,2,1,0:T(8,128)(2,1)}, bf16[4,256,3328]{2,1,0:T(8,128)(2,1)}, bf16[4,256,3328]{2,1,0:T(8,128)(2,1)}) custom-call(bf16[256,2048]{1,0:T(8,128)(2,1)} %tok_ref.1, bf16[256,6656]{1,0:T(8,128)(2,1)} %gate_ref.1, bf16[256,6656]{1,0:T(8,128)(2,1)} %up_ref.1), custom_call_target="tpu_custom_call" | custom-call | tf_op jit(solution)/shard_map/spread/pallas_call | solution.py:350
  176.2 29.1 %hidden.1 = (bf16[512,3328]{1,0:T(8,128)(2,1)S(1)}, bf16[4,512,1024]{2,1,0:T(8,128)(2,1)}) custom-call(s32[26,8]{1,0:T(8,128)S(1)} %copy.8.rows_ref, s32[1]{0:T(128)S(6)} %sub.12.begin_ref, bf16[8,2,256,2048]{3,2,1,0:T(8,128)(2,1)} %get-tuple-element.12.t_ref, bf16[1024,3328]{1,0:T(8,128)(2,1)} %bitcast.5, bf16[1024,3328]{1,0:T(8,128)(2,1)} %bitcast.6), custom_call_target="tpu_custom_call" | custom-call | tf_op jit(solution)/shard_map/hidden/pallas_call | solution.py:369
  205.3 0.0 copy-start.2
  205.3 2.2 copy-done.2
  207.5 138.7 %join.1 = (bf16[1024,6656]{1,0:T(8,128)(2,1)}, bf16[1024,1024]{1,0:T(8,128)(2,1)S(1)}) custom-call(bf16[512,3328]{1,0:T(8,128)(2,1)S(1)} %get-tuple-element.15.h_ref, bf16[4,512,1024]{2,1,0:T(8,128)(2,1)S(1)} %copy-done.2), custom_call_target="tpu_custom_call" | custom-call | tf_op jit(solution)/shard_map/join/pallas_call | solution.py:389
  346.2 0.0 copy-start.3
  346.2 1.3 copy-done.3
  347.5 2.9 copy.7
  350.4 0.0 copy-start.1
  350.4 23.5 %product.1 = f32[1024,6656]{1,0:T(8,128)} custom-call(bf16[1024,1024]{1,0:T(8,128)(2,1)S(1)} %bitcast.4, bf16[1024,6656]{1,0:T(8,128)(2,1)} %get-tuple-element.18.b_ref), custom_call_target="tpu_custom_call" | custom-call | tf_op jit(solution)/shard_map/product/pallas_call | solution.py:408
  373.9 0.0 copy-done.1
Async XLA Ops:
  0.0 0.7 copy-start
  205.3 2.2 copy-start.2
  346.2 1.3 copy-start.3
  350.4 23.5 %copy-start.1 = (s32[52,8]{0,1:T(8,128)S(1)}, s32[52,8]{0,1:T(8,128)}, u32[]{:S(2)}) copy-start(s32[52,8]{0,1:T(8,128)} %param.8) | copy-start | bytes 4996

commit v3 on v2

--- a/solution.py
+++ b/solution.py
@@ -44,11 +44,11 @@
            w_send, w_recv, l_sem, x_send, x_recv, c_send, c_recv, up_send, up_recv, dn_send, dn_recv):
     f, t, z, c, y, x = places()
     half = g_ref.shape[2]
-    xn, yn, dn = y * 2 + 1 - x, (1 - y) * 2 + x, (1 - y) * 2 + 1 - x
+    xn, yn = y * 2 + 1 - x, (1 - y) * 2 + x
     partner = z * 2 + 1 - c
     above, below = f + 2, f - 2
     greet(
-        [dict(tok=xn), dict(tok=yn), dict(tok=dn), dict(ffn=partner)],
+        [dict(tok=xn), dict(tok=yn), dict(ffn=partner)],
         [(z < chips - 1, dict(ffn=above)), (z > 0, dict(ffn=below))],
     )
     ends = []
@@ -77,24 +77,25 @@
         across(src, dst, zs, j).start()
 
     pass_on(tok_ref, own, z, 0, z < chips - 1, z > 0)
-    copies = []
-    for k, (there, x_there) in enumerate(((xn, 1 - x), (yn, x), (dn, 1 - x))):
-        cols = pl.ds(pl.multiple_of(x_there * half, BLOCK), half)
-        for m, (src, dst) in enumerate(((gate_ref, g_ref), (up_ref, u_ref))):
-            copy = remote(src.at[:, cols], dst.at[t], w_send.at[k, m], w_recv.at[k, m], tok=there)
-            copy.start()
-            copies.append(copy)
-    cols = pl.ds(pl.multiple_of(x * half, BLOCK), half)
+    here = pl.ds(pl.multiple_of(x * half, BLOCK), half)
+    there = pl.ds(pl.multiple_of((1 - x) * half, BLOCK), half)
+    pairs = ((gate_ref, g_ref), (up_ref, u_ref))
+    over_y = [remote(s.at[:, here], d.at[t], w_send.at[0, m], w_recv.at[0, m], tok=yn) for m, (s, d) in enumerate(pairs)]
+    over_x = [remote(s.at[:, there], d.at[t], w_send.at[1, m], w_recv.at[1, m], tok=xn) for m, (s, d) in enumerate(pairs)]
+    onward = [remote(d.at[xn], d.at[xn], w_send.at[2, m], w_recv.at[2, m], tok=yn) for m, (s, d) in enumerate(pairs)]
+    for copy in over_y:
+        copy.start()
     locals_ = [
         pltpu.make_async_copy(tok_ref, own, l_sem.at[0]),
-        pltpu.make_async_copy(gate_ref.at[:, cols], g_ref.at[t], l_sem.at[1]),
-        pltpu.make_async_copy(up_ref.at[:, cols], u_ref.at[t], l_sem.at[2]),
+        pltpu.make_async_copy(gate_ref.at[:, here], g_ref.at[t], l_sem.at[1]),
+        pltpu.make_async_copy(up_ref.at[:, here], u_ref.at[t], l_sem.at[2]),
     ]
     for copy in locals_:
         copy.start()
     other = t_ref.at[f, 1 - x]
     remote(tok_ref, other, x_send, x_recv, tok=xn).wait_recv()
     pass_on(other, other, z, 1, z < chips - 1, z > 0)
+    over_x[0].start()
     for k in range(1, chips):
         for j in range(2):
             xs = x if j == 0 else 1 - x
@@ -110,6 +111,13 @@
                 piece = t_ref.at[f + 2 * k, xs]
                 down(piece, piece, z + k, j).wait_recv()
                 pass_on(piece, piece, z + k, j, None, z > 0)
+
+        if k < 3:
+            over_x[k - 1].wait_recv()
+            onward[k - 1].start()
+            if k == 1:
+                over_x[0].wait_send()
+                over_x[1].start()
 
     for zs in range(chips):
         for j in range(2):
@@ -129,8 +137,9 @@
     cx.wait_send()
     for copy in locals_:
         copy.wait()
-    for copy in copies:
+    for copy in over_y + onward:
         copy.wait()
+    over_x[1].wait_send()
 
 
 CHUNKS = 4
@@ -150,16 +159,19 @@
     )
     cut = rows // 2
 
+    first = rows * 9 // 16
+    spans = ((0, first), (first, rows - first))
+
     def part(yy, xx, s):
         return p_ref.at[
-            pl.ds(pl.multiple_of(yy * rows + s * cut, 16), cut),
+            pl.ds(pl.multiple_of(yy * rows + spans[s][0], 16), spans[s][1]),
             pl.ds(pl.multiple_of(xx * half, BLOCK), half),
         ]
 
     def copy(src, yy, xx, s, n, there):
         return remote(src, part(yy, xx, s), send.at[n], recv.at[n], tok=there)
 
-    own = [h_ref.at[pl.ds(s * cut, cut)] for s in range(2)]
+    own = [h_ref.at[pl.ds(*span)] for span in spans]
     sent = [
         copy(own[0], y, x, 0, 0, xn), copy(own[1], y, x, 1, 2, yn),
         copy(own[1], y, x, 1, 1, xn), copy(own[0], y, x, 0, 3, yn),
@@ -306,33 +318,41 @@
 
 def hidden_kernel(per, rows_ref, begin_ref, t_ref, g_ref, u_ref, h_ref, s_ref):
     i = pl.program_id(0)
-    depth = g_ref.shape[0]
-    tiles = []
-    for k in range(depth // BLOCK):
-        r = rows_ref[i, k]
-        tile = t_ref[r // per, :, :, pl.ds(pl.multiple_of((r % per) * BLOCK, BLOCK), BLOCK)]
-        tiles.append(tile.reshape(-1, BLOCK))
-    picked = jnp.concatenate(tiles, axis=1)
-    weights = jnp.concatenate([g_ref[...], u_ref[...]], axis=1)
-    both = jnp.dot(picked, weights, preferred_element_type=jnp.float32)
-    gate, up = both[:, :BLOCK], both[:, BLOCK:]
-    hidden = (gate / (1.0 + jnp.exp(-gate)) * up).astype(h_ref.dtype)
-    h_ref[...] = hidden
+    depth, width = g_ref.shape
+    many = width // BLOCK
+    wide = s_ref.shape[2] // BLOCK
 
     @pl.when(i == 0)
     def _():
         s_ref[...] = jnp.zeros_like(s_ref)
 
-    wide = s_ref.shape[2] // BLOCK
-    at = i - begin_ref[0]
-
-    @pl.when((at >= 0) & (at < wide * s_ref.shape[0]))
+    for n in range(many):
+        column = i * many + n
+        span = pl.ds(n * BLOCK, BLOCK)
+        tiles = []
+        for k in range(depth // BLOCK):
+            r = rows_ref[column, k]
+            tile = t_ref[r // per, :, :, pl.ds(pl.multiple_of((r % per) * BLOCK, BLOCK), BLOCK)]
+            tiles.append(tile.reshape(-1, BLOCK))
+        picked = jnp.concatenate(tiles, axis=1)
+        weights = jnp.concatenate([g_ref[:, span], u_ref[:, span]], axis=1)
+        both = jnp.dot(picked, weights, preferred_element_type=jnp.float32)
+        gate, up = both[:, :BLOCK], both[:, BLOCK:]
+        hidden = (gate / (1.0 + jnp.exp(-gate)) * up).astype(h_ref.dtype)
+        h_ref[:, span] = hidden
+        at = column - begin_ref[0]
+
+        @pl.when((at >= 0) & (at < wide * s_ref.shape[0]))
+        def _():
+            s_ref[at // wide, :, pl.ds(pl.multiple_of((at % wide) * BLOCK, BLOCK), BLOCK)] = hidden
+
+
+def product_kernel(scale, a_ref, b_ref, o_ref, turned):
+    @pl.when(pl.program_id(0) == 0)
     def _():
-        s_ref[at // wide, :, pl.ds(pl.multiple_of((at % wide) * BLOCK, BLOCK), BLOCK)] = hidden
-
-
-def product_kernel(scale, a_ref, b_ref, o_ref):
-    o_ref[...] = jnp.dot(a_ref[...], b_ref[...], preferred_element_type=jnp.float32) * scale
+        turned[...] = a_ref[...].T
+
+    o_ref[...] = jnp.dot(turned[...], b_ref[...], preferred_element_type=jnp.float32) * scale
 
 
 def params(**more):
@@ -364,6 +384,7 @@
     f = lax.axis_index("ffn")
     count = half // BLOCK
     rows_here = lax.dynamic_slice_in_dim(block_rows, (t % 2) * count, count, 0)
+    many = 2 if count % 2 == 0 else 1
     wide = SLAB // 4
     begin = slab_offset // BLOCK - (f * 2 + t % 2) * count
     hidden, slab = pl.pallas_call(
@@ -371,14 +392,14 @@
         out_shape=(shape((2 * rows, half), bf), shape((4, 2 * rows, wide), bf)),
         grid_spec=pltpu.PrefetchScalarGridSpec(
             num_scalar_prefetch=2,
-            grid=(count,),
+            grid=(count // many,),
             in_specs=[
                 pl.BlockSpec(memory_space=pltpu.VMEM),
-                pl.BlockSpec((4 * depth, BLOCK), lambda i, r, b: (0, i)),
-                pl.BlockSpec((4 * depth, BLOCK), lambda i, r, b: (0, i)),
+                pl.BlockSpec((4 * depth, many * BLOCK), lambda i, r, b: (0, i)),
+                pl.BlockSpec((4 * depth, many * BLOCK), lambda i, r, b: (0, i)),
             ],
             out_specs=(
-                pl.BlockSpec((2 * rows, BLOCK), lambda i, r, b: (0, i)),
+                pl.BlockSpec((2 * rows, many * BLOCK), lambda i, r, b: (0, i)),
                 pl.BlockSpec((4, 2 * rows, wide), lambda i, r, b: (0, 0, 0)),
             ),
         ),
@@ -403,17 +424,17 @@
         ),
         name="join",
     )(hidden, slab)
-    row_panel = row_panel.T
     tile = 512 if panel % 512 == 0 else BLOCK
     return pl.pallas_call(
         functools.partial(product_kernel, 2.0 / (4 * rows)),
         out_shape=shape((wide, panel), jnp.float32),
         grid=(panel // tile,),
         in_specs=[
-            pl.BlockSpec((wide, 4 * rows), lambda i: (0, 0)),
+            pl.BlockSpec((4 * rows, wide), lambda i: (0, 0)),
             pl.BlockSpec((4 * rows, tile), lambda i: (0, i)),
         ],
         out_specs=pl.BlockSpec((wide, tile), lambda i: (0, i)),
+        scratch_shapes=[vmem((wide, 4 * rows), bf)],
         compiler_params=params(vmem_limit_bytes=48 * 1024 * 1024),
         name="product",
     )(row_panel, whole)
@@ -460,7 +481,7 @@
     ffn, tok = mesh.shape["ffn"], mesh.shape["tok"]
 
     def body(tokens, gate_blocks, up_blocks, block_rows, slab_offset):
-        if tok == 4 and ffn % 2 == 0 and block_rows.shape[0] % 2 == 0:
+        if tok == 4 and ffn >= 6 and ffn % 2 == 0 and block_rows.shape[0] % 2 == 0:
             return shards_split(ffn, tokens, gate_blocks, up_blocks, block_rows, slab_offset)
         return shards(tokens, gate_blocks, up_blocks, block_rows, slab_offset)
 

time: 375 us -> 347 us (0.925)
  Pallas kernels: 367 us -> 343 us
  local copies, waits for them, and re-layouts: 6.53 us -> 2.36 us
    pallas_call x1, Pallas kernels: 175 us -> 152 us  [shards_split(): pl.pallas_call(functools.partial(spread, chips), out_shape=(shape((ffn, 2...]
where the time goes in v3:
time: 347 us; the launch traced here: 346 us
  Pallas kernels  343 us (99%)
    pallas_call x1, Pallas kernels, shards_split(): pl.pallas_call(functools.partial(spread, chips), out_shape=(shape((ffn, 2...  152 us
    pallas_call x1, Pallas kernels, shards_split(): pl.pallas_call(functools.partial(join, chips), out_shape=(shape((4 * rows...  139 us
    pallas_call x1, Pallas kernels, shards_split(): pl.pallas_call(functools.partial(hidden_kernel, feats // BLOCK), out_shap...  28.3 us
    pallas_call x1, Pallas kernels, shards_split(): pl.pallas_call(functools.partial(product_kernel, 2.0 / (4 * rows)), out_s...  24.1 us

profile of v3, /device:TPU:0, one launch (start us, length us, event | category | flops | bytes accessed | tf_op | source)
XLA Modules:
  0.0 346.0 jit_solution(3893273485172373674)
XLA Ops:
  0.0 0.0 copy-start
  0.7 0.0 copy-done
  0.7 0.1 constant_dynamic-slice_fusion
  0.8 0.1 copy.7.rows_ref
  0.9 151.9 %spread.1 = (bf16[8,2,256,2048]{3,2,1,0:T(8,128)(2,1)}, bf16[4,256,3328]{2,1,0:T(8,128)(2,1)}, bf16[4,256,3328]{2,1,0:T(8,128)(2,1)}) custom-call(bf16[256,2048]{1,0:T(8,128)(2,1)} %tok_ref.1, bf16[256,6656]{1,0:T(8,128)(2,1)} %gate_ref.1, bf16[256,6656]{1,0:T(8,128)(2,1)} %up_ref.1), custom_call_target="tpu_custom_call" | custom-call | tf_op jit(solution)/shard_map/spread/pallas_call | solution.py:370
  152.8 28.3 %hidden.1 = (bf16[512,3328]{1,0:T(8,128)(2,1)S(1)}, bf16[4,512,1024]{2,1,0:T(8,128)(2,1)}) custom-call(s32[26,8]{1,0:T(8,128)S(1)} %copy.7.rows_ref, s32[1]{0:T(128)S(6)} %sub.12.begin_ref, bf16[8,2,256,2048]{3,2,1,0:T(8,128)(2,1)} %get-tuple-element.12.t_ref, bf16[1024,3328]{1,0:T(8,128)(2,1)} %bitcast.3, bf16[1024,3328]{1,0:T(8,128)(2,1)} %bitcast.4), custom_call_target="tpu_custom_call" | custom-call | tf_op jit(solution)/shard_map/hidden/pallas_call | solution.py:390
  181.0 0.0 copy-start.2
  181.0 2.2 copy-done.2
  183.2 138.7 %join.1 = (bf16[1024,6656]{1,0:T(8,128)(2,1)}, bf16[1024,1024]{1,0:T(8,128)(2,1)S(1)}) custom-call(bf16[512,3328]{1,0:T(8,128)(2,1)S(1)} %get-tuple-element.15.h_ref, bf16[4,512,1024]{2,1,0:T(8,128)(2,1)S(1)} %copy-done.2), custom_call_target="tpu_custom_call" | custom-call | tf_op jit(solution)/shard_map/join/pallas_call | solution.py:410
  321.9 0.0 copy-start.1
  321.9 24.1 %product.1 = f32[1024,6656]{1,0:T(8,128)} custom-call(bf16[1024,1024]{1,0:T(8,128)(2,1)S(1)} %get-tuple-element.17.a_ref, bf16[1024,6656]{1,0:T(8,128)(2,1)} %get-tuple-element.18.b_ref), custom_call_target="tpu_custom_call" | custom-call | tf_op jit(solution)/shard_map/product/pallas_call | solution.py:428
  346.0 0.0 copy-done.1
Async XLA Ops:
  0.0 0.7 copy-start
  181.0 2.2 copy-start.2
  321.9 24.1 %copy-start.1 = (s32[52,8]{0,1:T(8,128)S(1)}, s32[52,8]{0,1:T(8,128)}, u32[]{:S(2)}) copy-start(s32[52,8]{0,1:T(8,128)} %param.8) | copy-start | bytes 4996

commit v4 on v3

--- a/solution.py
+++ b/solution.py
@@ -263,7 +263,12 @@
     copy(via_x, y, 1 - x, 0, 0, xn).wait_recv()
     fy = copy(via_x, y, 1 - x, 0, 4, yn)
     fy.start()
-    line(2, CHUNKS + chips - 1)
+    line(2, 4)
+    via_y = part(1 - y, x, 1)
+    copy(via_y, 1 - y, x, 1, 2, yn).wait_recv()
+    fx = copy(via_y, 1 - y, x, 1, 5, xn)
+    fx.start()
+    line(4, CHUNKS + chips - 1)
 
     @pl.loop(0, CHUNKS)
     def _(k):
@@ -284,10 +289,6 @@
     to_core.start()
     keep = pltpu.make_async_copy(e.at[y], slab_rows(y), l_sem.at[2])
     keep.start()
-    via_y = part(1 - y, x, 1)
-    copy(via_y, 1 - y, x, 1, 2, yn).wait_recv()
-    fx = copy(via_y, 1 - y, x, 1, 5, xn)
-    fx.start()
     from_y = slab_rows(1 - y)
     remote(e.at[1 - y], from_y, r_send.at[0], r_recv.at[0], tok=yn).wait_recv()
     again = remote(from_y, from_y, r_send.at[2], r_recv.at[2], ffn=partner)

time: 347 us -> 339 us (0.977)
  Pallas kernels: 343 us -> 335 us
    pallas_call x1, Pallas kernels: 139 us -> 131 us  [shards_split(): pl.pallas_call(functools.partial(join, chips), out_shape=(shape((4 * rows...]
where the time goes in v4:
time: 339 us; the launch traced here: 338 us
  Pallas kernels  335 us (99%)
    pallas_call x1, Pallas kernels, shards_split(): pl.pallas_call(functools.partial(spread, chips), out_shape=(shape((ffn, 2...  152 us
    pallas_call x1, Pallas kernels, shards_split(): pl.pallas_call(functools.partial(join, chips), out_shape=(shape((4 * rows...  131 us
    pallas_call x1, Pallas kernels, shards_split(): pl.pallas_call(functools.partial(hidden_kernel, feats // BLOCK), out_shap...  28.3 us
    pallas_call x1, Pallas kernels, shards_split(): pl.pallas_call(functools.partial(product_kernel, 2.0 / (4 * rows)), out_s...  24.1 us

profile of v4, /device:TPU:0, one launch (start us, length us, event | category | flops | bytes accessed | tf_op | source)
XLA Modules:
  0.0 338.3 jit_solution(5495852609330184071)
XLA Ops:
  0.0 0.0 copy-start
  0.7 0.0 copy-done
  0.7 0.1 constant_dynamic-slice_fusion
  0.8 0.1 copy.7.rows_ref
  0.9 151.9 %spread.1 = (bf16[8,2,256,2048]{3,2,1,0:T(8,128)(2,1)}, bf16[4,256,3328]{2,1,0:T(8,128)(2,1)}, bf16[4,256,3328]{2,1,0:T(8,128)(2,1)}) custom-call(bf16[256,2048]{1,0:T(8,128)(2,1)} %tok_ref.1, bf16[256,6656]{1,0:T(8,128)(2,1)} %gate_ref.1, bf16[256,6656]{1,0:T(8,128)(2,1)} %up_ref.1), custom_call_target="tpu_custom_call" | custom-call | tf_op jit(solution)/shard_map/spread/pallas_call | solution.py:371
  152.8 28.3 %hidden.1 = (bf16[512,3328]{1,0:T(8,128)(2,1)S(1)}, bf16[4,512,1024]{2,1,0:T(8,128)(2,1)}) custom-call(s32[26,8]{1,0:T(8,128)S(1)} %copy.7.rows_ref, s32[1]{0:T(128)S(6)} %sub.12.begin_ref, bf16[8,2,256,2048]{3,2,1,0:T(8,128)(2,1)} %get-tuple-element.12.t_ref, bf16[1024,3328]{1,0:T(8,128)(2,1)} %bitcast.3, bf16[1024,3328]{1,0:T(8,128)(2,1)} %bitcast.4), custom_call_target="tpu_custom_call" | custom-call | tf_op jit(solution)/shard_map/hidden/pallas_call | solution.py:391
  181.0 0.0 copy-start.2
  181.1 2.2 copy-done.2
  183.2 131.0 %join.1 = (bf16[1024,6656]{1,0:T(8,128)(2,1)}, bf16[1024,1024]{1,0:T(8,128)(2,1)S(1)}) custom-call(bf16[512,3328]{1,0:T(8,128)(2,1)S(1)} %get-tuple-element.15.h_ref, bf16[4,512,1024]{2,1,0:T(8,128)(2,1)S(1)} %copy-done.2), custom_call_target="tpu_custom_call" | custom-call | tf_op jit(solution)/shard_map/join/pallas_call | solution.py:411
  314.2 0.0 copy-start.1
  314.2 24.1 %product.1 = f32[1024,6656]{1,0:T(8,128)} custom-call(bf16[1024,1024]{1,0:T(8,128)(2,1)S(1)} %get-tuple-element.17.a_ref, bf16[1024,6656]{1,0:T(8,128)(2,1)} %get-tuple-element.18.b_ref), custom_call_target="tpu_custom_call" | custom-call | tf_op jit(solution)/shard_map/product/pallas_call | solution.py:429
  338.3 0.0 copy-done.1
Async XLA Ops:
  0.0 0.7 copy-start
  181.0 2.2 copy-start.2
  314.2 24.1 %copy-start.1 = (s32[52,8]{0,1:T(8,128)S(1)}, s32[52,8]{0,1:T(8,128)}, u32[]{:S(2)}) copy-start(s32[52,8]{0,1:T(8,128)} %param.8) | copy-start | bytes 4996

commit v5 on v4

--- a/solution.py
+++ b/solution.py
@@ -404,7 +404,7 @@
                 pl.BlockSpec((4, 2 * rows, wide), lambda i, r, b: (0, 0, 0)),
             ),
         ),
-        compiler_params=params(vmem_limit_bytes=48 * 1024 * 1024),
+        compiler_params=params(vmem_limit_bytes=60 * 1024 * 1024),
         name="hidden",
     )(rows_here, begin, spread_tokens, gates.reshape(4 * depth, half), ups.reshape(4 * depth, half))
     vmem = pltpu.VMEM
@@ -421,7 +421,7 @@
             dma((3,)), dma((3,)),
         ],
         compiler_params=params(
-            collective_id=1, has_side_effects=True, vmem_limit_bytes=32 * 1024 * 1024
+            collective_id=1, has_side_effects=True, vmem_limit_bytes=60 * 1024 * 1024
         ),
         name="join",
     )(hidden, slab)
@@ -436,7 +436,7 @@
         ],
         out_specs=pl.BlockSpec((wide, tile), lambda i: (0, i)),
         scratch_shapes=[vmem((wide, 4 * rows), bf)],
-        compiler_params=params(vmem_limit_bytes=48 * 1024 * 1024),
+        compiler_params=params(vmem_limit_bytes=60 * 1024 * 1024),
         name="product",
     )(row_panel, whole)
 

time: 339 us -> 339 us (level)
  no operation moved by 1% of the time
where the time goes in v5:
time: 339 us; the launch traced here: 338 us
  Pallas kernels  336 us (99%)
    pallas_call x1, Pallas kernels, shards_split(): pl.pallas_call(functools.partial(spread, chips), out_shape=(shape((ffn, 2...  152 us
    pallas_call x1, Pallas kernels, shards_split(): pl.pallas_call(functools.partial(join, chips), out_shape=(shape((4 * rows...  131 us
    pallas_call x1, Pallas kernels, shards_split(): pl.pallas_call(functools.partial(hidden_kernel, feats // BLOCK), out_shap...  28.5 us
    pallas_call x1, Pallas kernels, shards_split(): pl.pallas_call(functools.partial(product_kernel, 2.0 / (4 * rows)), out_s...  24.8 us

profile of v5, /device:TPU:0, one launch (start us, length us, event | category | flops | bytes accessed | tf_op | source)
XLA Modules:
  0.0 337.7 jit_solution(11386355891926046201)
XLA Ops:
  0.0 0.0 copy-start
  0.7 0.0 copy-done
  0.7 0.1 constant_dynamic-slice_fusion
  0.8 0.7 copy.7.rows_ref
  1.5 151.9 %spread.1 = (bf16[8,2,256,2048]{3,2,1,0:T(8,128)(2,1)}, bf16[4,256,3328]{2,1,0:T(8,128)(2,1)}, bf16[4,256,3328]{2,1,0:T(8,128)(2,1)}) custom-call(bf16[256,2048]{1,0:T(8,128)(2,1)} %tok_ref.1, bf16[256,6656]{1,0:T(8,128)(2,1)} %gate_ref.1, bf16[256,6656]{1,0:T(8,128)(2,1)} %up_ref.1), custom_call_target="tpu_custom_call" | custom-call | tf_op jit(solution)/shard_map/spread/pallas_call | solution.py:371
  153.4 28.5 %hidden.1 = (bf16[512,3328]{1,0:T(8,128)(2,1)}, bf16[4,512,1024]{2,1,0:T(8,128)(2,1)}) custom-call(s32[26,8]{1,0:T(8,128)} %copy.7.rows_ref, s32[1]{0:T(128)S(6)} %sub.12.begin_ref, bf16[8,2,256,2048]{3,2,1,0:T(8,128)(2,1)} %get-tuple-element.12.t_ref, bf16[1024,3328]{1,0:T(8,128)(2,1)} %bitcast.3, bf16[1024,3328]{1,0:T(8,128)(2,1)} %bitcast.4), custom_call_target="tpu_custom_call" | custom-call | tf_op jit(solution)/shard_map/hidden/pallas_call | solution.py:391
  181.9 131.0 %join.1 = (bf16[1024,6656]{1,0:T(8,128)(2,1)}, bf16[1024,1024]{1,0:T(8,128)(2,1)}) custom-call(bf16[512,3328]{1,0:T(8,128)(2,1)} %get-tuple-element.15.h_ref, bf16[4,512,1024]{2,1,0:T(8,128)(2,1)} %get-tuple-element.16.s_ref), custom_call_target="tpu_custom_call" | custom-call | tf_op jit(solution)/shard_map/join/pallas_call | solution.py:411
  312.9 0.0 copy-start.1
  312.9 24.8 %product.1 = f32[1024,6656]{1,0:T(8,128)} custom-call(bf16[1024,1024]{1,0:T(8,128)(2,1)} %get-tuple-element.17.a_ref, bf16[1024,6656]{1,0:T(8,128)(2,1)} %get-tuple-element.18.b_ref), custom_call_target="tpu_custom_call" | custom-call | tf_op jit(solution)/shard_map/product/pallas_call | solution.py:429
  337.7 0.0 copy-done.1
Async XLA Ops:
  0.0 0.7 copy-start
  312.9 24.8 %copy-start.1 = (s32[52,8]{0,1:T(8,128)S(1)}, s32[52,8]{0,1:T(8,128)}, u32[]{:S(2)}) copy-start(s32[52,8]{0,1:T(8,128)} %param.8) | copy-start | bytes 4996
